TPU v7x, 256 devices: a whole 4x4x8 slice. The times are simulated.
256 devices in a mesh: adapter: 8 (over z), tensor: 32 (over y, x, core).
Axes of the slice: x: 4, y: 4, z: 8, core: 2. Of those that a mesh axis runs over, the one named last changes fastest.
Arguments:
- hidden_activations: bfloat16 [2048, 16384], P('adapter', 'tensor'), may hold values from -6 to 6
- cotangent: bfloat16 [2048, 8192], P('adapter'), may hold values from -1.5 to 1.5
- shadow_assignment: int32 [2048], P('adapter'), may hold values from 0 to 63, as said below
- frozen_down_weight: bfloat16 [16384, 8192], P('tensor'), may hold values from -0.046875 to 0.046875
- adapter_down_factors: bfloat16 [64, 16, 16384], P('adapter', None, 'tensor'), may hold values from -0.046875 to 0.046875
- adapter_up_factors: bfloat16 [64, 16, 8192], P('adapter', None, 'tensor'), may hold values from -1.5 to 1.5
Outputs:
- mixed: bfloat16 [2048, 8192], P('adapter')
- hidden_input_gradient: bfloat16 [2048, 16384], P('adapter', 'tensor')
- down_factor_gradient: float32 [64, 16, 16384], P('adapter', None, 'tensor')
- up_factor_gradient: float32 [64, 16, 8192], P('adapter', None, 'tensor')
Inputs may be any that keep to these rules, and one draw needn't show every extreme that they name: `shadow_assignment`: the shadows fall into groups of 8 consecutive numbers. Among the 256 tokens of each aligned block (the tokens of one device) at most 128 belong to one group; one group, the same in every block, has exactly 128 tokens in every block.
All inputs are finite; a program needn't handle non-finite values.
Results may differ from a plain program's by a relative error of at most 0.0038.
Values may be sent and summed in bfloat16 or wider, within the bound.
A program may use at most 128 MiB of HBM per device.

v0:
```python
import jax
import jax.numpy as jnp
from jax import lax
from jax.sharding import PartitionSpec as P


def contract_rows(left, right):
    return lax.dot_general(
        left, right, (((0,), (0,)), ((), ())), preferred_element_type=jnp.float32
    )


def contract_cols(left, right):
    return lax.dot_general(
        left, right, (((1,), (1,)), ((), ())), preferred_element_type=jnp.float32
    )


def adapter_contributions(row_acts, row_grads, local_ids, down_table, up_table):
    shadow_count, low_rank, width_ff = down_table.shape
    width_model = up_table.shape[2]
    row_total = row_acts.shape[0]
    selector = local_ids[:, None] == jnp.arange(shadow_count, dtype=jnp.int32)[None, :]
    select_f = selector.astype(jnp.float32)
    select_b = selector.astype(jnp.bfloat16)
    down_factor_flat = down_table.reshape(shadow_count * low_rank, width_ff)
    up_factor_flat = up_table.reshape(shadow_count * low_rank, width_model)
    low_all = contract_cols(row_acts, down_factor_flat).reshape(row_total, shadow_count, low_rank)
    back_all = contract_cols(row_grads, up_factor_flat).reshape(row_total, shadow_count, low_rank)
    low_part = jnp.sum(low_all * select_f[:, :, None], axis=1)
    back_part = jnp.sum(back_all * select_f[:, :, None], axis=1)
    low_sum, back_sum = lax.psum((low_part, back_part), "tensor")
    reduced_sparse_rows = (select_b[:, :, None] * low_sum.astype(jnp.bfloat16)[:, None, :]).reshape(
        row_total, shadow_count * low_rank
    )
    backward_sparse_rows = (
        select_b[:, :, None] * back_sum.astype(jnp.bfloat16)[:, None, :]
    ).reshape(row_total, shadow_count * low_rank)
    adapter_output = jnp.dot(
        reduced_sparse_rows, up_factor_flat, preferred_element_type=jnp.float32
    )
    adapter_backward = jnp.dot(
        backward_sparse_rows, down_factor_flat, preferred_element_type=jnp.float32
    )
    down_factor_piece = contract_rows(backward_sparse_rows, row_acts).reshape(
        shadow_count, low_rank, width_ff
    )
    up_factor_piece = contract_rows(reduced_sparse_rows, row_grads).reshape(
        shadow_count, low_rank, width_model
    )
    return (adapter_output, adapter_backward, down_factor_piece, up_factor_piece)


def on_device(
    hidden_activations,
    cotangent,
    shadow_assignment,
    frozen_down_weight,
    adapter_down_factors,
    adapter_up_factors,
):
    tensor_count = lax.axis_size("tensor")
    tensor_position = lax.axis_index("tensor")
    token_count = hidden_activations.shape[0]
    width_model = cotangent.shape[1]
    local_hidden_width = width_model // tensor_count
    grad_local = lax.dynamic_slice_in_dim(
        cotangent, tensor_position * local_hidden_width, local_hidden_width, 1
    )
    frozen_output = jnp.dot(
        hidden_activations, frozen_down_weight, preferred_element_type=jnp.float32
    )
    frozen_backward = contract_cols(cotangent, frozen_down_weight)
    group_number = lax.axis_size("adapter")
    tokens_per_group = adapter_down_factors.shape[0]
    slot_capacity = token_count // 2
    slot_overall_count = group_number * slot_capacity
    owners = shadow_assignment // tokens_per_group
    local_ids = shadow_assignment - owners * tokens_per_group
    owner_hot = (owners[:, None] == jnp.arange(group_number, dtype=jnp.int32)[None, :]).astype(
        jnp.int32
    )
    earlier = jnp.cumsum(owner_hot, axis=0) - owner_hot
    slot_position_index = owners * slot_capacity + jnp.sum(earlier * owner_hot, axis=1)
    slot_match = (
        slot_position_index[None, :] == jnp.arange(slot_overall_count, dtype=jnp.int32)[:, None]
    )
    placement_map = slot_match.astype(jnp.bfloat16)
    packed_acts = jnp.dot(placement_map, hidden_activations, preferred_element_type=jnp.bfloat16)
    packed_grads = jnp.dot(placement_map, grad_local, preferred_element_type=jnp.bfloat16)
    packed_ids = jnp.sum(jnp.where(slot_match, local_ids[None, :] + 1, 0), axis=1) - 1
    recv_acts, recv_grads, recv_ids = (
        lax.all_to_all(
            packed_acts.reshape(group_number, slot_capacity, -1),
            "adapter",
            split_axis=0,
            concat_axis=0,
            tiled=True,
        ),
        lax.all_to_all(
            packed_grads.reshape(group_number, slot_capacity, -1),
            "adapter",
            split_axis=0,
            concat_axis=0,
            tiled=True,
        ),
        lax.all_to_all(
            packed_ids.reshape(group_number, slot_capacity),
            "adapter",
            split_axis=0,
            concat_axis=0,
            tiled=True,
        ),
    )
    adapter_slot_rows, backward_slot_rows, down_factor_gradient, up_factor_gradient = (
        adapter_contributions(
            recv_acts.reshape(slot_overall_count, -1),
            recv_grads.reshape(slot_overall_count, -1),
            recv_ids.reshape(slot_overall_count),
            adapter_down_factors,
            adapter_up_factors,
        )
    )
    output_returned, backward_returned = (
        lax.all_to_all(
            adapter_slot_rows.reshape(group_number, slot_capacity, -1),
            "adapter",
            split_axis=0,
            concat_axis=0,
            tiled=True,
        ),
        lax.all_to_all(
            backward_slot_rows.reshape(group_number, slot_capacity, -1),
            "adapter",
            split_axis=0,
            concat_axis=0,
            tiled=True,
        ),
    )
    adapter_output = jnp.take(
        output_returned.reshape(slot_overall_count, -1), slot_position_index, axis=0
    )
    adapter_backward = jnp.take(
        backward_returned.reshape(slot_overall_count, -1), slot_position_index, axis=0
    )
    own_cols = (
        lax.dynamic_slice_in_dim(
            frozen_output, tensor_position * local_hidden_width, local_hidden_width, 1
        )
        + adapter_output
    )
    partial_out = lax.dynamic_update_slice_in_dim(
        frozen_output, own_cols, tensor_position * local_hidden_width, 1
    )
    mixed = lax.psum(partial_out, "tensor").astype(jnp.bfloat16)
    hidden_input_gradient = (frozen_backward + adapter_backward).astype(jnp.bfloat16)
    return (mixed, hidden_input_gradient, down_factor_gradient, up_factor_gradient)


def solution(mesh):
    return jax.shard_map(
        on_device,
        mesh=mesh,
        in_specs=(
            P("adapter", "tensor"),
            P("adapter", None),
            P("adapter"),
            P("tensor", None),
            P("adapter", None, "tensor"),
            P("adapter", None, "tensor"),
        ),
        out_specs=(
            P("adapter", None),
            P("adapter", "tensor"),
            P("adapter", None, "tensor"),
            P("adapter", None, "tensor"),
        ),
        check_vma=False,
    )
```

profile of v0, /device:TPU:1, one launch (start us, length us, event | category | flops | bytes accessed | tf_op | source)
XLA Modules:
  0.0 451.8 jit_solution(5459070656954331394)
XLA Ops:
  0.6 0.7 subtract_add_fusion
  3.2 9.0 %all-to-all-start = ((s32[8,1,128]{2,1,0:T(1,128)}), s32[8,1,128]{2,1,0:T(1,128)S(1)}, u32[]{:S(2)}, u32[]{:S(2)}) async-start(s32[8,1,128]{2,1,0:T(1,128)} %bitcast.3), calls=%async_computation | async-start | bytes 8192 | tf_op jit(solution)/shard_map/all_to_all | solution.py:107
  12.2 1.4 fusion.4
  13.6 5.0 %all-to-all-done = s32[8,1,128]{2,1,0:T(1,128)S(1)} async-done(((s32[8,1,128]{2,1,0:T(1,128)}), s32[8,1,128]{2,1,0:T(1,128)S(1)}, u32[]{:S(2)}, u32[]{:S(2)}) %all-to-all-start) | async-done | bytes 4128 | tf_op jit(solution)/shard_map/all_to_all | solution.py:107
  18.6 3.6 all-to-all-start.1
  22.2 2.0 fusion.3
  24.2 27.1 %all-to-all-done.1 = bf16[8,128,512]{2,1,0:T(8,128)(2,1)S(1)} async-done(((bf16[8,128,512]{2,1,0:T(8,128)(2,1)}), bf16[8,128,512]{2,1,0:T(8,128)(2,1)S(1)}, u32[]{:S(2)}, u32[]{:S(2)}) %all-to-all-start.1) | async-done | bytes 1048608 | tf_op jit(solution)/shard_map/all_to_all | solution.py:93
  51.3 3.5 all-to-all-start.3
  54.8 1.4 fusion.2
  56.2 123.8 %psum.21 = bf16[1024,16]{0,1:T(8,128)(2,1)S(1)} all-reduce(f32[1024,16]{0,1:T(8,128)S(1)} %fusion.2), channel_id=1, replica_groups=mesh['adapter'=8,'tensor'=32] {'tensor'}, use_global_device_ids=true, to_apply=%region_5.6 | all-reduce | flops 16384 | bytes 98304 | tf_op jit(solution)/shard_map/psum | solution.py:32
  180.1 2.1 fusion.13
  182.2 6.2 %all-to-all-start.2 = ((f32[8,128,256]{2,1,0:T(8,128)}), f32[8,128,256]{2,1,0:T(8,128)S(1)}, u32[]{:S(2)}, u32[]{:S(2)}) async-start(f32[8,128,256]{2,1,0:T(8,128)} %fusion.13), calls=%async_computation.2 | async-start | bytes 2097152 | tf_op jit(solution)/shard_map/all_to_all | solution.py:125
  188.4 9.0 %fusion.22 = f32[256,8192]{1,0:T(8,128)} fusion(bf16[256,512]{1,0:T(8,128)(2,1)S(1)} %copy-done, bf16[512,8192]{1,0:T(8,128)(2,1)} %param.9), kind=kOutput, calls=%fused_computation.47 | convolution fusion | flops 2147483648 | bytes 17039360 | tf_op jit(solution)/shard_map/dot_general | solution.py:70
  197.7 15.8 %all-to-all-done.2 = f32[8,128,256]{2,1,0:T(8,128)S(1)} async-done(((f32[8,128,256]{2,1,0:T(8,128)}), f32[8,128,256]{2,1,0:T(8,128)S(1)}, u32[]{:S(2)}, u32[]{:S(2)}) %all-to-all-start.2) | async-done | bytes 1048608 | tf_op jit(solution)/shard_map/all_to_all | solution.py:125
  213.5 1.0 gather_fusion
  214.5 1.8 add_dynamic-update-slice_fusion
  216.3 175.0 %all-reduce.2 = (bf16[256,8192]{1,0:T(8,128)(2,1)}, bf16[1024,16]{0,1:T(8,128)(2,1)S(1)}) all-reduce(f32[256,8192]{1,0:T(8,128)} %add_dynamic-update-slice_fusion, f32[1024,16]{0,1:T(8,128)S(1)} %fusion.1), channel_id=1, replica_groups=mesh['adapter'=8,'tensor'=32] {'tensor'}, use_global_device_ids=true, to_apply=%region_6.7 | all-reduce | flops 2113536 | bytes 12681216 | tf_op jit(solution)/shard_map/psum | solution.py:155
  391.4 1.8 fusion.11
  393.2 3.6 all-to-all-start.4
  396.8 1.9 fusion.7
  398.7 1.0 fusion.9
  399.7 43.3 %all-to-all-done.4 = f32[8,128,512]{2,1,0:T(8,128)S(1)} async-done(((f32[8,128,512]{2,1,0:T(8,128)}), f32[8,128,512]{2,1,0:T(8,128)S(1)}, u32[]{:S(2)}, u32[]{:S(2)}) %all-to-all-start.4) | async-done | bytes 2097184 | tf_op jit(solution)/shard_map/all_to_all | solution.py:132
  443.0 1.0 gather_fusion.1
  444.0 7.7 %fusion = bf16[256,512]{1,0:T(8,128)(2,1)} fusion(bf16[256,8192]{1,0:T(8,128)(2,1)} %param.7, bf16[512,8192]{1,0:T(8,128)(2,1)} %param.9, f32[256,512]{1,0:T(8,128)S(1)} %gather_fusion.1, pred[256]{0:T(512)(128)(4,1)S(1)} %get-tuple-element.6), kind=kOutput, calls=%fused_computation.5 | convolution fusion | flops 2147876864 | bytes 13369600 | tf_op jit(solution)/shard_map/dot_general | solution.py:14
  (26 shorter events, 2.2 us)
Async XLA Ops:
  0.6 11.5 %copy-start = (bf16[256,512]{1,0:T(8,128)(2,1)S(1)}, bf16[256,512]{1,0:T(8,128)(2,1)}, u32[]{:S(2)}) copy-start(bf16[256,512]{1,0:T(8,128)(2,1)} %param.6) | copy-start | bytes 786436
  3.2 15.5 %all-to-all-start = ((s32[8,1,128]{2,1,0:T(1,128)}), s32[8,1,128]{2,1,0:T(1,128)S(1)}, u32[]{:S(2)}, u32[]{:S(2)}) async-start(s32[8,1,128]{2,1,0:T(1,128)} %bitcast.3), calls=%async_computation | async-start | bytes 8192 | tf_op jit(solution)/shard_map/all_to_all | solution.py:107
  18.6 32.7 %all-to-all-start.1 = ((bf16[8,128,512]{2,1,0:T(8,128)(2,1)}), bf16[8,128,512]{2,1,0:T(8,128)(2,1)S(1)}, u32[]{:S(2)}, u32[]{:S(2)}) async-start(bf16[8,128,512]{2,1,0:T(8,128)(2,1)} %bitcast.5), calls=%async_computation.1 | async-start | bytes 2097152 | tf_op jit(solution)/shard_map/all_to_all | solution.py:93
  51.3 131.0 %all-to-all-start.3 = ((bf16[8,128,256]{2,1,0:T(8,128)(2,1)}), bf16[8,128,256]{2,1,0:T(8,128)(2,1)S(1)}, u32[]{:S(2)}, u32[]{:S(2)}) async-start(bf16[8,128,256]{2,1,0:T(8,128)(2,1)} %bitcast.11), calls=%async_computation.3 | async-start | bytes 1048576 | tf_op jit(solution)/shard_map/all_to_all | solution.py:100
  182.2 15.2 %copy-start.1 = (bf16[8,128,256]{2,1,0:T(8,128)(2,1)}, bf16[8,128,256]{2,1,0:T(8,128)(2,1)S(1)}, u32[]{:S(2)}) copy-start(bf16[8,128,256]{2,1,0:T(8,128)(2,1)S(1)} %all-to-all-done.3) | copy-start | bytes 1572868
  182.2 31.3 %all-to-all-start.2 = ((f32[8,128,256]{2,1,0:T(8,128)}), f32[8,128,256]{2,1,0:T(8,128)S(1)}, u32[]{:S(2)}, u32[]{:S(2)}) async-start(f32[8,128,256]{2,1,0:T(8,128)} %fusion.13), calls=%async_computation.2 | async-start | bytes 2097152 | tf_op jit(solution)/shard_map/all_to_all | solution.py:125
  188.4 9.0 %copy-start.3 = (bf16[8,16,256]{2,1,0:T(8,128)(2,1)S(1)}, bf16[8,16,256]{2,1,0:T(8,128)(2,1)}, u32[]{:S(2)}) copy-start(bf16[8,16,256]{2,1,0:T(8,128)(2,1)} %param.11) | copy-start | bytes 196612
  197.4 193.9 %copy-start.2 = (bf16[8,16,512]{2,1,0:T(8,128)(2,1)S(1)}, bf16[8,16,512]{2,1,0:T(8,128)(2,1)}, u32[]{:S(2)}) copy-start(bf16[8,16,512]{2,1,0:T(8,128)(2,1)} %param.10) | copy-start | bytes 393220
  393.2 49.9 %all-to-all-start.4 = ((f32[8,128,512]{2,1,0:T(8,128)}), f32[8,128,512]{2,1,0:T(8,128)S(1)}, u32[]{:S(2)}, u32[]{:S(2)}) async-start(f32[8,128,512]{2,1,0:T(8,128)} %fusion.11), calls=%async_computation.4 | async-start | bytes 4194304 | tf_op jit(solution)/shard_map/all_to_all | solution.py:132
where the time goes:
time: 457 us; the launch traced here: 452 us
  blocking collectives  299 us (65%)
  waiting for transfers between devices  91.2 us (20%)
  matrix products  28.7 us (6%)
  starting transfers between devices  25.8 us (6%)
    psum x1, blocking collectives, on_device(): mixed = lax.psum(partial_out, 'tensor').astype(jnp.bfloat16)  175 us
    psum x1, blocking collectives, adapter_contributions(): low_sum, back_sum = lax.psum((low_part, back_part), 'tensor')  124 us
    all_to_all x1, waiting for transfers between devices, on_device(): lax.all_to_all(backward_slot_rows.reshape(group_number, slot_capacity, -1...  43.3 us
    all_to_all x1, waiting for transfers between devices, on_device(): lax.all_to_all(packed_acts.reshape(group_number, slot_capacity, -1), 'ada...  27.1 us
    all_to_all x1, waiting for transfers between devices, on_device(): lax.all_to_all(adapter_slot_rows.reshape(group_number, slot_capacity, -1)...  15.8 us
    dot_general x3, matrix products, contract_cols(): lax.dot_general(left, right, (((1,), (1,)), ((), ())), preferred_element_...  9.42 us
  transfers between devices with their start and end apart: 5, of which 4 were waited for; matrix products, arithmetic and copies ran while one was open for 4% of the time, Pallas kernels for 0%

commit v1 on v0

v1 whole, which is shorter than its diff:
```python
import jax
import jax.numpy as jnp
from jax import lax
from jax.experimental import pallas as pl
from jax.experimental.pallas import tpu as pltpu
from jax.sharding import PartitionSpec as P

BF = jnp.bfloat16
F32 = jnp.float32
MESH = pl.DeviceIdType.MESH
NSEM = 160
OFFS = (2, 1, 3, 0)


def nt(left, right):
    return lax.dot_general(left, right, (((1,), (1,)), ((), ())), preferred_element_type=F32)


def tn(left, right):
    return lax.dot_general(left, right, (((0,), (0,)), ((), ())), preferred_element_type=F32)


def nn(left, right):
    return lax.dot_general(left, right, (((1,), (0,)), ((), ())), preferred_element_type=F32)


def kernel(
    x_hbm, g_hbm, ids_ref, w_hbm, ad_hbm, au_hbm,
    mixed, hg_out, dg_out, ug_out,
    xv, gs, gv, wv, adv, auv,
    own, sib_tx, sib_rx, rs_tx, rs_rx, r_buf, p2_tx, p2_rx, fb,
    hg_acc, hg_bf, lr_acc, lr_tx, lr_rx, sel, zr_own, zr_tx, zr_rx, dg_buf, ug_buf,
    lsem, wsem, gsem, ssem, rsem,
):
    z = lax.axis_index("adapter")
    t = lax.axis_index("tensor")
    c = lax.rem(t, 2)
    x = lax.rem(lax.div(t, 2), 4)
    y = lax.div(t, 8)
    d = 1 - c
    p = x * d + y * c
    q = y * d + x * c

    def tid(pp, qq, cc):
        return lax.rem(pp, 4) * (2 + 6 * cc) + lax.rem(qq, 4) * (8 - 6 * cc) + cc

    def cols(block):
        return pl.ds(pl.multiple_of(block * 256, 256), 256)

    sib = (z, t + 1 - 2 * c)

    def at_p(k):
        return (z, tid(p + k, q, c))

    def at_q(k):
        return (z, tid(p, q + k, c))

    def at_x(k):
        return (z, (y * 4 + lax.rem(x + k, 4)) * 2 + c)

    def at_y(k):
        return (z, (lax.rem(y + k, 4) * 4 + x) * 2 + c)

    zp = (lax.rem(z + 1, 8), t)
    zm = (lax.rem(z + 7, 8), t)

    def slot(k):
        return lax.rem(z + k + 8, 8)

    count = [0]
    sent = []

    def send(src, dst, device):
        i = count[0]
        count[0] += 1
        cp = pltpu.make_async_remote_copy(
            src_ref=src, dst_ref=dst, send_sem=ssem.at[i], recv_sem=rsem.at[i],
            device_id=device, device_id_type=MESH,
        )
        cp.start()
        sent.append(cp)
        return cp

    def load(src, dst, sem):
        cp = pltpu.make_async_copy(src, dst, sem)
        cp.start()
        return cp

    ld_x = load(x_hbm, xv, lsem.at[0])

    def group_block(g, j):
        k, mine = g // 2, g % 2
        if mine:
            return tid(p + OFFS[k], j, c)
        return tid(q + OFFS[k], j, d)

    ld_w = [
        [load(w_hbm.at[:, cols(group_block(g, j))], wv.at[g, :, pl.ds(j * 256, 256)], wsem.at[g * 4 + j])
         for j in range(4)] for g in range(8)
    ]
    ld_ad = load(ad_hbm, adv.at[z], lsem.at[1])
    ld_au = load(au_hbm, auv.at[z], lsem.at[2])
    ld_gs = load(g_hbm.at[:, cols(t)], gs, lsem.at[3])
    ld_g = [
        [load(g_hbm.at[:, cols(group_block(g, j))], gv.at[g, :, pl.ds(j * 256, 256)], gsem.at[g * 4 + j])
         for j in range(4)] for g in range(8)
    ]

    bar = pltpu.get_barrier_semaphore()
    for dev in [sib, zp, zm] + [at_x(k) for k in (1, 2, 3)] + [at_y(k) for k in (1, 2, 3)]:
        pl.semaphore_signal(bar, inc=1, device_id=dev, device_id_type=MESH)

    def matmul_round(k):
        for mine in (0, 1):
            g = 2 * k + mine
            for cp in ld_w[g]:
                cp.wait()

            def body(j, carry):
                at = pl.ds(pl.multiple_of(j * 256, 256), 256)
                res = nn(xv[...], wv[g, :, at])
                if mine:
                    own[k, :, at] = res
                else:
                    sib_tx[k, :, at] = res.astype(BF)
                return carry

            lax.fori_loop(0, 4, body, 0)

    ld_x.wait()
    matmul_round(0)
    pl.semaphore_wait(bar, 9)

    def ad0(s, rows=slice(None)):
        return adv.at[s, rows, pl.ds(0, 256)]

    def ad1(s, rows=slice(None)):
        return adv.at[s, rows, pl.ds(256, 256)]

    def au0(s, rows=slice(None)):
        return auv.at[s, rows, :]

    TOP, LOW = pl.ds(0, 64), pl.ds(64, 64)

    def ag_first(view, hbm):
        return send(hbm, view(z), zp), send(hbm, view(z), zm)

    def ag_next(view, prev, k):
        prev[0].wait_recv()
        prev[1].wait_recv()
        if k == 5:
            return None
        if k == 4:
            return (
                send(view(slot(-3), TOP), view(slot(-3), TOP), zp),
                send(view(slot(3), LOW), view(slot(3), LOW), zm),
            )
        a, b = slot(1 - k), slot(k - 1)
        return send(view(a), view(a), zp), send(view(b), view(b), zm)

    h0 = ag_first(ad0, ad_hbm.at[:, pl.ds(0, 256)])
    h1 = ag_first(ad1, ad_hbm.at[:, pl.ds(256, 256)])
    hu = ag_first(au0, au_hbm)

    def sib_send(k):
        return send(sib_tx.at[k], sib_rx.at[k], sib)

    def sib_add(k):
        own[k] = own[k] + sib_rx[k].astype(F32)

    s0 = sib_send(0)
    matmul_round(1)
    s1 = sib_send(1)
    s0.wait_recv()
    rs_tx[0] = (own[0, 0:128] + sib_rx[0, 0:128].astype(F32)).astype(BF)
    a_p = send(rs_tx.at[0], rs_rx.at[0], at_p(1))
    rs_tx[1] = (own[0, 128:256] + sib_rx[0, 128:256].astype(F32)).astype(BF)
    a_m = send(rs_tx.at[1], rs_rx.at[1], at_p(3))
    matmul_round(2)
    s2 = sib_send(2)
    h0 = ag_next(ad0, h0, 2)
    s1.wait_recv()
    sib_add(1)
    rs_tx[2] = own[1, 128:256].astype(BF)
    b_p = send(rs_tx.at[2], rs_rx.at[2], at_p(1))
    h1 = ag_next(ad1, h1, 2)
    s2.wait_recv()
    sib_add(2)
    rs_tx[3] = own[2, 0:128].astype(BF)
    b_m = send(rs_tx.at[3], rs_rx.at[3], at_p(3))
    matmul_round(3)
    s3 = sib_send(3)
    hu = ag_next(au0, hu, 2)

    def mask(s):
        want = lax.broadcasted_iota(jnp.int32, (8, 1, 256), 0) + s * 8
        return want == ids_ref[...].reshape(1, 1, 256)

    def project(which, s):
        if which == 0:
            full = nt(adv[s], xv[...])
        else:
            full = nt(auv[s], gs[...])
        lr_acc[which] += jnp.sum(jnp.where(mask(s), full.reshape(8, 16, 256), 0.0), axis=0)

    lr_acc[...] = jnp.zeros_like(lr_acc)
    ld_ad.wait()
    project(0, z)
    s3.wait_recv()
    sib_add(3)
    a_p.wait_recv()
    rs_tx[4] = (own[1, 0:128] + rs_rx[0].astype(F32)).astype(BF)
    c_p = send(rs_tx.at[4], rs_rx.at[4], at_p(1))
    a_m.wait_recv()
    rs_tx[5] = (own[2, 128:256] + rs_rx[1].astype(F32)).astype(BF)
    c_m = send(rs_tx.at[5], rs_rx.at[5], at_p(3))
    h0 = ag_next(ad0, h0, 3)
    project(0, slot(1))
    project(0, slot(7))

    def backward(lo, hi, first):
        for g in range(lo, hi):
            for cp in ld_g[g]:
                cp.wait()
        if first:
            hg_acc[...] = jnp.zeros_like(hg_acc)

        def body(g, carry):
            hg_acc[...] += nt(gv[g], wv[g])
            return carry

        lax.fori_loop(lo, hi, body, 0)

    backward(0, 2, True)
    h1 = ag_next(ad1, h1, 3)
    project(0, slot(2))
    project(0, slot(6))
    hu = ag_next(au0, hu, 3)
    backward(2, 4, False)
    h0 = ag_next(ad0, h0, 4)
    b_m.wait_recv()
    b_p.wait_recv()
    c_p.wait_recv()
    r_buf[0:128] = own[3, 0:128] + rs_rx[3].astype(F32) + rs_rx[4].astype(F32)
    c_m.wait_recv()
    r_buf[128:256] = own[3, 128:256] + rs_rx[2].astype(F32) + rs_rx[5].astype(F32)

    p2 = []
    for k in (1, 3, 2):
        p2_tx[k - 1] = r_buf[:, cols(lax.rem(q + k, 4))].astype(BF)
        p2.append(send(p2_tx.at[k - 1], p2_rx.at[k - 1], at_q(k)))
    h1 = ag_next(ad1, h1, 4)
    project(0, slot(3))
    project(0, slot(5))
    hu = ag_next(au0, hu, 4)
    h0 = ag_next(ad0, h0, 5)
    h1 = ag_next(ad1, h1, 5)
    project(0, slot(4))

    def psum_start(which, stage):
        lr_tx[which, stage] = lr_acc[which]
        src = lr_tx.at[which, stage]
        if stage == 0:
            return [send(src, lr_rx.at[which, 0], sib)]
        at = at_x if stage == 1 else at_y
        return [send(src, lr_rx.at[which, 3 * stage - 3 + k], at(k)) for k in (1, 2, 3)]

    def psum_end(which, stage, cps):
        for cp in cps:
            cp.wait_recv()
        if stage == 0:
            lr_acc[which] += lr_rx[which, 0]
        else:
            b = 3 * stage - 3
            lr_acc[which] += lr_rx[which, b + 1] + lr_rx[which, b + 2] + lr_rx[which, b + 3]

    lp = psum_start(0, 0)
    ld_au.wait()
    ld_gs.wait()
    project(1, z)
    project(1, slot(1))
    project(1, slot(7))
    psum_end(0, 0, lp)
    lp = psum_start(0, 1)
    project(1, slot(2))
    project(1, slot(6))
    project(1, slot(3))
    project(1, slot(5))
    backward(4, 6, False)
    for cp in p2:
        cp.wait_recv()
    hu = ag_next(au0, hu, 5)
    project(1, slot(4))
    bp = psum_start(1, 0)
    psum_end(0, 1, lp)
    lp = psum_start(0, 2)
    psum_end(1, 0, bp)
    bp = psum_start(1, 1)
    backward(6, 8, False)
    f_pre = (
        r_buf[:, cols(q)] + p2_rx[0].astype(F32) + p2_rx[1].astype(F32) + p2_rx[2].astype(F32)
    )
    r_buf[:, 0:256] = f_pre
    psum_end(0, 2, lp)

    def select(which):
        low = lr_acc[which].astype(BF).astype(F32)[None]
        for s in range(8):
            sel[which, pl.ds(s * 128, 128)] = (
                jnp.where(mask(s), low, 0.0).reshape(128, 256).astype(BF)
            )

    select(0)
    adapted = tn(sel[0], auv[...].reshape(1024, 256))
    fb[...] = (r_buf[:, 0:256] + adapted).astype(BF)

    def gather(block, device, rows=slice(None)):
        ref = mixed.at[rows, cols(block)]
        return send(ref, ref, device)

    mine = tid(p, q, c)
    own_out = mixed.at[:, cols(mine)]
    ag_p = {}
    ag_m = {}
    ag_p[0] = send(fb, own_out, at_p(1))
    ag_m[0] = send(fb, own_out, at_p(3))
    ag_q = {k: send(fb, own_out, at_q(k)) for k in (1, 3, 2)}
    sibs = [send(fb, own_out, sib)]
    ld_own = load(fb, own_out, lsem.at[4])

    def grad_part(chain, s):
        rows = pl.ds(pl.multiple_of(s * 128, 128), 128)
        if chain == 0:
            return nn(sel[0, rows], gs[...])
        return nn(sel[1, rows], xv[:, (chain - 1) * 256:chain * 256])

    def rs_start(chain):
        zr_tx[chain, 0] = grad_part(chain, slot(4)).astype(BF)
        hp = send(zr_tx.at[chain, 0, TOP], zr_rx.at[chain, 0, TOP], zp)
        hm = send(zr_tx.at[chain, 0, LOW], zr_rx.at[chain, 0, LOW], zm)
        for k in (3, 2, 1):
            zr_own[chain, 3 - k] = grad_part(chain, slot(k))
            zr_own[chain, 6 - k] = grad_part(chain, slot(-k))
        zr_own[chain, 6] = grad_part(chain, z)
        return hp, hm

    def rs_next(chain, step, prev):
        prev[0].wait_recv()
        if step == 1:
            zr_tx[chain, 1, TOP] = (zr_own[chain, 0, TOP] + zr_rx[chain, 0, TOP].astype(F32)).astype(BF)
            zr_tx[chain, 1, LOW] = zr_own[chain, 0, LOW].astype(BF)
        else:
            zr_tx[chain, step] = (zr_own[chain, step - 1] + zr_rx[chain, step - 1].astype(F32)).astype(BF)
        hp = send(zr_tx.at[chain, step], zr_rx.at[chain, step], zp)
        prev[1].wait_recv()
        if step == 1:
            zr_tx[chain, 4, TOP] = zr_own[chain, 3, TOP].astype(BF)
            zr_tx[chain, 4, LOW] = (zr_own[chain, 3, LOW] + zr_rx[chain, 0, LOW].astype(F32)).astype(BF)
        else:
            zr_tx[chain, 3 + step] = (
                zr_own[chain, 2 + step] + zr_rx[chain, 2 + step].astype(F32)
            ).astype(BF)
        hm = send(zr_tx.at[chain, 3 + step], zr_rx.at[chain, 3 + step], zm)
        return hp, hm

    def rs_end(chain, prev):
        prev[0].wait_recv()
        prev[1].wait_recv()
        return zr_own[chain, 6] + zr_rx[chain, 3].astype(F32) + zr_rx[chain, 6].astype(F32)

    cu = rs_start(0)
    psum_end(1, 1, bp)
    bp = psum_start(1, 2)

    def spread(k):
        ag_p[k].wait_recv()
        bm = tid(p + 3, q + k, c)
        f1 = gather(bm, at_p(1), pl.ds(0, 128))
        sibs.append(gather(bm, sib))
        ag_m[k].wait_recv()
        bq = tid(p + 1, q + k, c)
        f2 = gather(bq, at_p(3), pl.ds(128, 128))
        sibs.append(gather(bq, sib))
        return f1, f2

    halves = {}
    halves[0] = spread(0)
    for k in (1, 3, 2):
        ag_q[k].wait_recv()
        blk = tid(p, q + 4 - k, c)
        ag_p[4 - k] = gather(blk, at_p(1))
        ag_m[4 - k] = gather(blk, at_p(3))
        sibs.append(gather(blk, sib))
        if k == 3:
            cu = rs_next(0, 1, cu)
    psum_end(1, 2, bp)
    select(1)
    c0 = rs_start(1)
    c1 = rs_start(2)
    hg_bf[...] = (hg_acc[...] + tn(sel[1], adv[...].reshape(1024, 512))).astype(BF)
    st_hg = load(hg_bf, hg_out, lsem.at[5])
    cu = rs_next(0, 2, cu)
    halves[3] = spread(3)
    c0 = rs_next(1, 1, c0)
    c1 = rs_next(2, 1, c1)
    halves[1] = spread(1)
    cu = rs_next(0, 3, cu)
    c0 = rs_next(1, 2, c0)
    c1 = rs_next(2, 2, c1)
    halves[2] = spread(2)
    for k in (0, 3, 1, 2):
        f1, f2 = halves[k]
        blk = tid(p + 2, q + k, c)
        f1.wait_recv()
        f2.wait_recv()
        sibs.append(gather(blk, sib))
    ug_buf[...] = rs_end(0, cu)
    st_ug = load(ug_buf, ug_out, lsem.at[6])
    c0 = rs_next(1, 3, c0)
    c1 = rs_next(2, 3, c1)
    for cp in sibs:
        cp.wait_recv()
    dg_buf[:, 0:256] = rs_end(1, c0)
    dg_buf[:, 256:512] = rs_end(2, c1)
    st_dg = load(dg_buf, dg_out, lsem.at[7])
    for cp in sent:
        cp.wait_send()
    for cp in (ld_own, st_hg, st_ug, st_dg):
        cp.wait()


def on_device(x, g, ids, w, ad, au):
    any_spec = pl.BlockSpec(memory_space=pl.ANY)
    vmem = pl.BlockSpec(memory_space=pltpu.VMEM)
    mixed, hg, dg, ug = pl.pallas_call(
        kernel,
        out_shape=(
            jax.ShapeDtypeStruct((256, 8192), BF),
            jax.ShapeDtypeStruct((256, 512), BF),
            jax.ShapeDtypeStruct((128, 512), F32),
            jax.ShapeDtypeStruct((128, 256), F32),
        ),
        in_specs=[any_spec, any_spec, vmem, any_spec, any_spec, any_spec],
        out_specs=(any_spec,) * 4,
        scratch_shapes=[
            pltpu.VMEM((256, 512), BF),
            pltpu.VMEM((256, 256), BF),
            pltpu.VMEM((8, 256, 1024), BF),
            pltpu.VMEM((8, 512, 1024), BF),
            pltpu.VMEM((8, 128, 512), BF),
            pltpu.VMEM((8, 128, 256), BF),
            pltpu.VMEM((4, 256, 1024), F32),
            pltpu.VMEM((4, 256, 1024), BF),
            pltpu.VMEM((4, 256, 1024), BF),
            pltpu.VMEM((6, 128, 1024), BF),
            pltpu.VMEM((6, 128, 1024), BF),
            pltpu.VMEM((256, 1024), F32),
            pltpu.VMEM((3, 256, 256), BF),
            pltpu.VMEM((3, 256, 256), BF),
            pltpu.VMEM((256, 256), BF),
            pltpu.VMEM((256, 512), F32),
            pltpu.VMEM((256, 512), BF),
            pltpu.VMEM((2, 16, 256), F32),
            pltpu.VMEM((2, 3, 16, 256), F32),
            pltpu.VMEM((2, 7, 16, 256), F32),
            pltpu.VMEM((2, 1024, 256), BF),
            pltpu.VMEM((3, 7, 128, 256), F32),
            pltpu.VMEM((3, 7, 128, 256), BF),
            pltpu.VMEM((3, 7, 128, 256), BF),
            pltpu.VMEM((128, 512), F32),
            pltpu.VMEM((128, 256), F32),
            pltpu.SemaphoreType.DMA((8,)),
            pltpu.SemaphoreType.DMA((32,)),
            pltpu.SemaphoreType.DMA((32,)),
            pltpu.SemaphoreType.DMA((NSEM,)),
            pltpu.SemaphoreType.DMA((NSEM,)),
        ],
        compiler_params=pltpu.CompilerParams(
            collective_id=0, has_side_effects=True, vmem_limit_bytes=56 * 2**20
        ),
    )(x, g, ids.reshape(1, 256), w, ad.reshape(128, 512), au.reshape(128, 256))
    return mixed, hg, dg.reshape(8, 16, 512), ug.reshape(8, 16, 256)


def solution(mesh):
    return jax.shard_map(
        on_device,
        mesh=mesh,
        in_specs=(
            P("adapter", "tensor"),
            P("adapter", None),
            P("adapter"),
            P("tensor", None),
            P("adapter", None, "tensor"),
            P("adapter", None, "tensor"),
        ),
        out_specs=(
            P("adapter", None),
            P("adapter", "tensor"),
            P("adapter", None, "tensor"),
            P("adapter", None, "tensor"),
        ),
        check_vma=False,
    )
```

time: 457 us -> 78.4 us (0.17)
  blocking collectives: 299 us -> 0 us
  waiting for transfers between devices: 91.2 us -> 0 us
  Pallas kernels: 0 us -> 69.6 us
  matrix products: 28.7 us -> 0 us
  starting transfers between devices: 25.8 us -> 0 us
    psum x2 -> x0, blocking collectives: 299 us -> none  [the longest x1 175 us: on_device(): mixed = lax.psum(partial_out, 'tensor').astype(jnp.bfloat16)]
    all_to_all x5 -> x0, waiting for transfers between devices: 91.2 us -> none  [the longest x1 43.3 us: on_device(): lax.all_to_all(backward_slot_rows.reshape(group_number, slot_capacity, -1...]
    pallas_call x0 -> x1, Pallas kernels: none -> 69.6 us  [on_device(): pl.pallas_call(kernel, out_shape=(jax.ShapeDtypeStruct((256, 8192), BF),...]
    dot_general x10 -> x0, matrix products: 28.7 us -> none  [the longest x3 9.42 us: contract_cols(): lax.dot_general(left, right, (((1,), (1,)), ((), ())), preferred_element_...]
    all_to_all x5 -> x0, starting transfers between devices: 25.8 us -> none  [the longest x1 9.01 us: on_device(): lax.all_to_all(packed_ids.reshape(group_number, slot_capacity), 'adapter'...]
    unnamed x10, local copies, waits for them, and re-layouts: 0.11 us -> 6.77 us
  transfers between devices with their start and end apart: 5 -> 0, of which waited for: 4 -> 0; matrix products, arithmetic and copies ran while one was open for 4% -> 0% of each run, Pallas kernels for 0% -> 0%
where the time goes in v1:
time: 78.4 us; the launch traced here: 77 us
  Pallas kernels  69.6 us (89%)
  local copies, waits for them, and re-layouts  6.77 us (9%)
    pallas_call x1, Pallas kernels, on_device(): pl.pallas_call(kernel, out_shape=(jax.ShapeDtypeStruct((256, 8192), BF),...  69.6 us
    unnamed x10, local copies, waits for them, and re-layouts  6.77 us

profile of v1, /device:TPU:1, one launch (start us, length us, event | category | flops | bytes accessed | tf_op | source)
XLA Modules:
  0.0 77.0 jit_solution(7765483529015306604)
XLA Ops:
  0.6 69.6 %shard_map.93 = (bf16[256,8192]{1,0:T(8,128)(2,1)}, bf16[256,512]{1,0:T(8,128)(2,1)}, f32[128,512]{1,0:T(8,128)}, f32[128,256]{1,0:T(8,128)}) custom-call(bf16[256,512]{1,0:T(8,128)(2,1)} %x_hbm.1, bf16[256,8192]{1,0:T(8,128)(2,1)} %g_hbm.1, s32[1,256]{1,0:T(1,128)} %bitcast.9, bf16[512,8192]{1,0:T(8,128)(2,1)} %w_hbm.1, bf16[128,512]{1,0:T(8,128)(2,1)} %bitcast.6, ...), custom_call_target="tpu_custom_call" | custom-call | tf_op jit(solution)/shard_map/pallas_call | solution.py:435
  70.2 0.0 copy-start.1
  70.2 0.0 copy-start
  70.2 0.0 copy-start.2
  70.2 4.7 %copy.14 = bf16[256,8192]{1,0:T(8,128)(2,1)} copy(bf16[256,8192]{1,0:T(8,128)(2,1)} %get-tuple-element.16) | data formatting | bytes 8388608
  74.9 0.0 copy-done.1
  74.9 0.7 copy.15
  75.6 0.0 copy-done
  75.6 0.7 copy.16
  76.4 0.0 copy-done.2
  76.4 0.7 copy.17
Async XLA Ops:
  70.2 4.7 %copy-start.1 = (bf16[256,512]{1,0:T(8,128)(2,1)S(1)}, bf16[256,512]{1,0:T(8,128)(2,1)}, u32[]{:S(2)}) copy-start(bf16[256,512]{1,0:T(8,128)(2,1)} %get-tuple-element.17) | copy-start | bytes 786436
  70.2 5.4 %copy-start = (f32[128,512]{1,0:T(8,128)S(1)}, f32[128,512]{1,0:T(8,128)}, u32[]{:S(2)}) copy-start(f32[128,512]{1,0:T(8,128)} %get-tuple-element.10) | copy-start | bytes 786436
  70.2 6.1 %copy-start.2 = (f32[128,256]{1,0:T(8,128)S(1)}, f32[128,256]{1,0:T(8,128)}, u32[]{:S(2)}) copy-start(f32[128,256]{1,0:T(8,128)} %get-tuple-element.11) | copy-start | bytes 393220

commit v2 on v1

--- a/solution.py
+++ b/solution.py
@@ -94,41 +94,37 @@
             return tid(p + OFFS[k], j, c)
         return tid(q + OFFS[k], j, d)
 
-    ld_w = [
-        [load(w_hbm.at[:, cols(group_block(g, j))], wv.at[g, :, pl.ds(j * 256, 256)], wsem.at[g * 4 + j])
-         for j in range(4)] for g in range(8)
-    ]
-    ld_ad = load(ad_hbm, adv.at[z], lsem.at[1])
-    ld_au = load(au_hbm, auv.at[z], lsem.at[2])
-    ld_gs = load(g_hbm.at[:, cols(t)], gs, lsem.at[3])
-    ld_g = [
-        [load(g_hbm.at[:, cols(group_block(g, j))], gv.at[g, :, pl.ds(j * 256, 256)], gsem.at[g * 4 + j])
-         for j in range(4)] for g in range(8)
-    ]
+    def load_w(g):
+        return [
+            load(w_hbm.at[:, cols(group_block(g, j))], wv.at[g, :, pl.ds(j * 256, 256)], wsem.at[g * 4 + j])
+            for j in range(4)
+        ]
+
+    def load_g(g):
+        return [
+            load(g_hbm.at[:, cols(group_block(g, j))], gv.at[g, :, pl.ds(j * 256, 256)], gsem.at[g * 4 + j])
+            for j in range(4)
+        ]
+
+    ld_w = [load_w(0), load_w(1)]
 
     bar = pltpu.get_barrier_semaphore()
     for dev in [sib, zp, zm] + [at_x(k) for k in (1, 2, 3)] + [at_y(k) for k in (1, 2, 3)]:
         pl.semaphore_signal(bar, inc=1, device_id=dev, device_id_type=MESH)
 
-    def matmul_round(k):
-        for mine in (0, 1):
-            g = 2 * k + mine
-            for cp in ld_w[g]:
-                cp.wait()
-
-            def body(j, carry):
-                at = pl.ds(pl.multiple_of(j * 256, 256), 256)
-                res = nn(xv[...], wv[g, :, at])
-                if mine:
-                    own[k, :, at] = res
-                else:
-                    sib_tx[k, :, at] = res.astype(BF)
-                return carry
-
-            lax.fori_loop(0, 4, body, 0)
-
-    ld_x.wait()
-    matmul_round(0)
+    def matmul_half(k, mine):
+        g = 2 * k + mine
+        for cp in ld_w[g]:
+            cp.wait()
+
+        for j in range(2):
+            at = pl.ds(j * 512, 512)
+            res = nn(xv[...], wv[g, :, at])
+            if mine:
+                own[k, :, at] = res
+            else:
+                sib_tx[k, :, at] = res.astype(BF)
+
     pl.semaphore_wait(bar, 9)
 
     def ad0(s, rows=slice(None)):
@@ -158,39 +154,9 @@
         a, b = slot(1 - k), slot(k - 1)
         return send(view(a), view(a), zp), send(view(b), view(b), zm)
 
-    h0 = ag_first(ad0, ad_hbm.at[:, pl.ds(0, 256)])
-    h1 = ag_first(ad1, ad_hbm.at[:, pl.ds(256, 256)])
-    hu = ag_first(au0, au_hbm)
-
-    def sib_send(k):
+    def sib_part(k):
+        matmul_half(k, 0)
         return send(sib_tx.at[k], sib_rx.at[k], sib)
-
-    def sib_add(k):
-        own[k] = own[k] + sib_rx[k].astype(F32)
-
-    s0 = sib_send(0)
-    matmul_round(1)
-    s1 = sib_send(1)
-    s0.wait_recv()
-    rs_tx[0] = (own[0, 0:128] + sib_rx[0, 0:128].astype(F32)).astype(BF)
-    a_p = send(rs_tx.at[0], rs_rx.at[0], at_p(1))
-    rs_tx[1] = (own[0, 128:256] + sib_rx[0, 128:256].astype(F32)).astype(BF)
-    a_m = send(rs_tx.at[1], rs_rx.at[1], at_p(3))
-    matmul_round(2)
-    s2 = sib_send(2)
-    h0 = ag_next(ad0, h0, 2)
-    s1.wait_recv()
-    sib_add(1)
-    rs_tx[2] = own[1, 128:256].astype(BF)
-    b_p = send(rs_tx.at[2], rs_rx.at[2], at_p(1))
-    h1 = ag_next(ad1, h1, 2)
-    s2.wait_recv()
-    sib_add(2)
-    rs_tx[3] = own[2, 0:128].astype(BF)
-    b_m = send(rs_tx.at[3], rs_rx.at[3], at_p(3))
-    matmul_round(3)
-    s3 = sib_send(3)
-    hu = ag_next(au0, hu, 2)
 
     def mask(s):
         want = lax.broadcasted_iota(jnp.int32, (8, 1, 256), 0) + s * 8
@@ -203,21 +169,6 @@
             full = nt(auv[s], gs[...])
         lr_acc[which] += jnp.sum(jnp.where(mask(s), full.reshape(8, 16, 256), 0.0), axis=0)
 
-    lr_acc[...] = jnp.zeros_like(lr_acc)
-    ld_ad.wait()
-    project(0, z)
-    s3.wait_recv()
-    sib_add(3)
-    a_p.wait_recv()
-    rs_tx[4] = (own[1, 0:128] + rs_rx[0].astype(F32)).astype(BF)
-    c_p = send(rs_tx.at[4], rs_rx.at[4], at_p(1))
-    a_m.wait_recv()
-    rs_tx[5] = (own[2, 128:256] + rs_rx[1].astype(F32)).astype(BF)
-    c_m = send(rs_tx.at[5], rs_rx.at[5], at_p(3))
-    h0 = ag_next(ad0, h0, 3)
-    project(0, slot(1))
-    project(0, slot(7))
-
     def backward(lo, hi, first):
         for g in range(lo, hi):
             for cp in ld_g[g]:
@@ -231,77 +182,107 @@
 
         lax.fori_loop(lo, hi, body, 0)
 
-    backward(0, 2, True)
-    h1 = ag_next(ad1, h1, 3)
-    project(0, slot(2))
-    project(0, slot(6))
-    hu = ag_next(au0, hu, 3)
-    backward(2, 4, False)
-    h0 = ag_next(ad0, h0, 4)
-    b_m.wait_recv()
-    b_p.wait_recv()
-    c_p.wait_recv()
-    r_buf[0:128] = own[3, 0:128] + rs_rx[3].astype(F32) + rs_rx[4].astype(F32)
-    c_m.wait_recv()
-    r_buf[128:256] = own[3, 128:256] + rs_rx[2].astype(F32) + rs_rx[5].astype(F32)
-
-    p2 = []
-    for k in (1, 3, 2):
-        p2_tx[k - 1] = r_buf[:, cols(lax.rem(q + k, 4))].astype(BF)
-        p2.append(send(p2_tx.at[k - 1], p2_rx.at[k - 1], at_q(k)))
-    h1 = ag_next(ad1, h1, 4)
-    project(0, slot(3))
-    project(0, slot(5))
-    hu = ag_next(au0, hu, 4)
-    h0 = ag_next(ad0, h0, 5)
-    h1 = ag_next(ad1, h1, 5)
-    project(0, slot(4))
-
-    def psum_start(which, stage):
-        lr_tx[which, stage] = lr_acc[which]
-        src = lr_tx.at[which, stage]
+    def psum_start(stage):
+        lr_tx[stage] = lr_acc[...]
+        src = lr_tx.at[stage]
         if stage == 0:
-            return [send(src, lr_rx.at[which, 0], sib)]
+            return [send(src, lr_rx.at[0], sib)]
         at = at_x if stage == 1 else at_y
-        return [send(src, lr_rx.at[which, 3 * stage - 3 + k], at(k)) for k in (1, 2, 3)]
-
-    def psum_end(which, stage, cps):
+        return [send(src, lr_rx.at[3 * stage - 3 + k], at(k)) for k in (1, 3, 2)]
+
+    def psum_end(stage, cps):
         for cp in cps:
             cp.wait_recv()
         if stage == 0:
-            lr_acc[which] += lr_rx[which, 0]
+            lr_acc[...] += lr_rx[0]
         else:
             b = 3 * stage - 3
-            lr_acc[which] += lr_rx[which, b + 1] + lr_rx[which, b + 2] + lr_rx[which, b + 3]
-
-    lp = psum_start(0, 0)
+            lr_acc[...] += lr_rx[b + 1] + lr_rx[b + 2] + lr_rx[b + 3]
+
+    h0 = ag_first(ad0, ad_hbm.at[:, pl.ds(0, 256)])
+    ld_w += [load_w(g) for g in range(2, 8)]
+    ld_x.wait()
+    s0 = sib_part(0)
+    matmul_half(0, 1)
+    h1 = ag_first(ad1, ad_hbm.at[:, pl.ds(256, 256)])
+    s1 = sib_part(1)
+    matmul_half(1, 1)
+    hu = ag_first(au0, au_hbm)
+    ld_ad = load(ad_hbm, adv.at[z], lsem.at[1])
+    ld_au = load(au_hbm, auv.at[z], lsem.at[2])
+    ld_gs = load(g_hbm.at[:, cols(t)], gs, lsem.at[3])
+
+    def rs_send(k):
+        rs_tx[k] = (own[k] + sib_rx[k].astype(F32)).astype(BF)
+        return send(rs_tx.at[k], rs_rx.at[k], at_p(OFFS[k]))
+
+    s0.wait_recv()
+    a0 = rs_send(0)
+    s2 = sib_part(2)
+    h0 = ag_next(ad0, h0, 2)
+    matmul_half(2, 1)
+    s1.wait_recv()
+    a1 = rs_send(1)
+    h1 = ag_next(ad1, h1, 2)
+    s3 = sib_part(3)
+    s2.wait_recv()
+    a2 = rs_send(2)
+    hu = ag_next(au0, hu, 2)
+    lr_acc[...] = jnp.zeros_like(lr_acc)
+    ld_ad.wait()
+    ld_g = [load_g(g) for g in range(8)]
+    project(0, z)
+    h0 = ag_next(ad0, h0, 3)
+    matmul_half(3, 1)
+    project(0, slot(1))
+    h1 = ag_next(ad1, h1, 3)
     ld_au.wait()
     ld_gs.wait()
+    project(0, slot(7))
     project(1, z)
+    project(0, slot(2))
+    hu = ag_next(au0, hu, 3)
+    project(0, slot(6))
+    h0 = ag_next(ad0, h0, 4)
+    s3.wait_recv()
+    own[3] = own[3] + sib_rx[3].astype(F32)
+    h1 = ag_next(ad1, h1, 4)
     project(1, slot(1))
     project(1, slot(7))
-    psum_end(0, 0, lp)
-    lp = psum_start(0, 1)
+    project(0, slot(3))
+    hu = ag_next(au0, hu, 4)
+    project(0, slot(5))
+    h0 = ag_next(ad0, h0, 5)
     project(1, slot(2))
     project(1, slot(6))
+    h1 = ag_next(ad1, h1, 5)
+    project(0, slot(4))
     project(1, slot(3))
     project(1, slot(5))
-    backward(4, 6, False)
+    hu = ag_next(au0, hu, 5)
+    project(1, slot(4))
+    lp = psum_start(0)
+    a0.wait_recv()
+    own[3] = own[3] + rs_rx[0].astype(F32)
+    psum_end(0, lp)
+    lp = psum_start(1)
+    a1.wait_recv()
+    a2.wait_recv()
+    r_buf[...] = own[3] + (rs_rx[1].astype(F32) + rs_rx[2].astype(F32))
+    p2 = []
+    for k in (2, 1, 3):
+        p2_tx[k - 1] = r_buf[:, cols(lax.rem(q + k, 4))].astype(BF)
+        p2.append(send(p2_tx.at[k - 1], p2_rx.at[k - 1], at_q(k)))
+    backward(0, 3, True)
+    psum_end(1, lp)
+    lp = psum_start(2)
+    backward(3, 8, False)
     for cp in p2:
         cp.wait_recv()
-    hu = ag_next(au0, hu, 5)
-    project(1, slot(4))
-    bp = psum_start(1, 0)
-    psum_end(0, 1, lp)
-    lp = psum_start(0, 2)
-    psum_end(1, 0, bp)
-    bp = psum_start(1, 1)
-    backward(6, 8, False)
-    f_pre = (
+    r_buf[:, 0:256] = (
         r_buf[:, cols(q)] + p2_rx[0].astype(F32) + p2_rx[1].astype(F32) + p2_rx[2].astype(F32)
     )
-    r_buf[:, 0:256] = f_pre
-    psum_end(0, 2, lp)
+    psum_end(2, lp)
 
     def select(which):
         low = lr_acc[which].astype(BF).astype(F32)[None]
@@ -322,10 +303,8 @@
     own_out = mixed.at[:, cols(mine)]
     ag_p = {}
     ag_m = {}
-    ag_p[0] = send(fb, own_out, at_p(1))
-    ag_m[0] = send(fb, own_out, at_p(3))
     ag_q = {k: send(fb, own_out, at_q(k)) for k in (1, 3, 2)}
-    sibs = [send(fb, own_out, sib)]
+    sibs = []
     ld_own = load(fb, own_out, lsem.at[4])
 
     def grad_part(chain, s):
@@ -338,11 +317,12 @@
         zr_tx[chain, 0] = grad_part(chain, slot(4)).astype(BF)
         hp = send(zr_tx.at[chain, 0, TOP], zr_rx.at[chain, 0, TOP], zp)
         hm = send(zr_tx.at[chain, 0, LOW], zr_rx.at[chain, 0, LOW], zm)
-        for k in (3, 2, 1):
+        return hp, hm
+
+    def rs_parts(chain, ks):
+        for k in ks:
             zr_own[chain, 3 - k] = grad_part(chain, slot(k))
             zr_own[chain, 6 - k] = grad_part(chain, slot(-k))
-        zr_own[chain, 6] = grad_part(chain, z)
-        return hp, hm
 
     def rs_next(chain, step, prev):
         prev[0].wait_recv()
@@ -368,10 +348,6 @@
         prev[1].wait_recv()
         return zr_own[chain, 6] + zr_rx[chain, 3].astype(F32) + zr_rx[chain, 6].astype(F32)
 
-    cu = rs_start(0)
-    psum_end(1, 1, bp)
-    bp = psum_start(1, 2)
-
     def spread(k):
         ag_p[k].wait_recv()
         bm = tid(p + 3, q + k, c)
@@ -383,41 +359,57 @@
         sibs.append(gather(bq, sib))
         return f1, f2
 
-    halves = {}
-    halves[0] = spread(0)
-    for k in (1, 3, 2):
+    def pass_on(k):
         ag_q[k].wait_recv()
         blk = tid(p, q + 4 - k, c)
         ag_p[4 - k] = gather(blk, at_p(1))
         ag_m[4 - k] = gather(blk, at_p(3))
         sibs.append(gather(blk, sib))
-        if k == 3:
-            cu = rs_next(0, 1, cu)
-    psum_end(1, 2, bp)
+
+    def to_sib(k):
+        for cp in halves[k]:
+            cp.wait_recv()
+        sibs.append(gather(tid(p + 2, q + k, c), sib))
+
+    halves = {}
+    cu = rs_start(0)
     select(1)
+    ag_p[0] = send(fb, own_out, at_p(1))
+    ag_m[0] = send(fb, own_out, at_p(3))
+    sibs.append(send(fb, own_out, sib))
     c0 = rs_start(1)
     c1 = rs_start(2)
+    for chain in range(3):
+        rs_parts(chain, (3,))
+    cu = rs_next(0, 1, cu)
+    halves[0] = spread(0)
+    c0 = rs_next(1, 1, c0)
+    c1 = rs_next(2, 1, c1)
+    pass_on(1)
+    pass_on(3)
+    pass_on(2)
+    for chain in range(3):
+        rs_parts(chain, (2,))
     hg_bf[...] = (hg_acc[...] + tn(sel[1], adv[...].reshape(1024, 512))).astype(BF)
     st_hg = load(hg_bf, hg_out, lsem.at[5])
     cu = rs_next(0, 2, cu)
+    to_sib(0)
+    c0 = rs_next(1, 2, c0)
     halves[3] = spread(3)
-    c0 = rs_next(1, 1, c0)
-    c1 = rs_next(2, 1, c1)
+    c1 = rs_next(2, 2, c1)
+    for chain in range(3):
+        rs_parts(chain, (1,))
+        zr_own[chain, 6] = grad_part(chain, z)
     halves[1] = spread(1)
+    halves[2] = spread(2)
     cu = rs_next(0, 3, cu)
-    c0 = rs_next(1, 2, c0)
-    c1 = rs_next(2, 2, c1)
-    halves[2] = spread(2)
-    for k in (0, 3, 1, 2):
-        f1, f2 = halves[k]
-        blk = tid(p + 2, q + k, c)
-        f1.wait_recv()
-        f2.wait_recv()
-        sibs.append(gather(blk, sib))
+    c0 = rs_next(1, 3, c0)
+    to_sib(3)
+    c1 = rs_next(2, 3, c1)
+    to_sib(1)
+    to_sib(2)
     ug_buf[...] = rs_end(0, cu)
     st_ug = load(ug_buf, ug_out, lsem.at[6])
-    c0 = rs_next(1, 3, c0)
-    c1 = rs_next(2, 3, c1)
     for cp in sibs:
         cp.wait_recv()
     dg_buf[:, 0:256] = rs_end(1, c0)
@@ -429,17 +421,36 @@
         cp.wait()
 
 
+def hand_over(*refs):
+    sources, results, held, sems = refs[:4], refs[4:8], refs[8:12], refs[12]
+    pieces = [(0, pl.ds(i * 32, 32)) for i in range(8)] + [(i, slice(None)) for i in (1, 2, 3)]
+    inward = []
+    for n, (i, rows) in enumerate(pieces):
+        cp = pltpu.make_async_copy(sources[i].at[rows], held[i].at[rows], sems.at[0, n])
+        cp.start()
+        inward.append(cp)
+    outward = []
+    for n, (i, rows) in enumerate(pieces):
+        inward[n].wait()
+        cp = pltpu.make_async_copy(held[i].at[rows], results[i].at[rows], sems.at[1, n])
+        cp.start()
+        outward.append(cp)
+    for cp in outward:
+        cp.wait()
+
+
 def on_device(x, g, ids, w, ad, au):
     any_spec = pl.BlockSpec(memory_space=pl.ANY)
     vmem = pl.BlockSpec(memory_space=pltpu.VMEM)
-    mixed, hg, dg, ug = pl.pallas_call(
+    shapes = (
+        jax.ShapeDtypeStruct((256, 8192), BF),
+        jax.ShapeDtypeStruct((256, 512), BF),
+        jax.ShapeDtypeStruct((128, 512), F32),
+        jax.ShapeDtypeStruct((128, 256), F32),
+    )
+    landed = pl.pallas_call(
         kernel,
-        out_shape=(
-            jax.ShapeDtypeStruct((256, 8192), BF),
-            jax.ShapeDtypeStruct((256, 512), BF),
-            jax.ShapeDtypeStruct((128, 512), F32),
-            jax.ShapeDtypeStruct((128, 256), F32),
-        ),
+        out_shape=shapes,
         in_specs=[any_spec, any_spec, vmem, any_spec, any_spec, any_spec],
         out_specs=(any_spec,) * 4,
         scratch_shapes=[
@@ -452,8 +463,8 @@
             pltpu.VMEM((4, 256, 1024), F32),
             pltpu.VMEM((4, 256, 1024), BF),
             pltpu.VMEM((4, 256, 1024), BF),
-            pltpu.VMEM((6, 128, 1024), BF),
-            pltpu.VMEM((6, 128, 1024), BF),
+            pltpu.VMEM((3, 256, 1024), BF),
+            pltpu.VMEM((3, 256, 1024), BF),
             pltpu.VMEM((256, 1024), F32),
             pltpu.VMEM((3, 256, 256), BF),
             pltpu.VMEM((3, 256, 256), BF),
@@ -461,8 +472,8 @@
             pltpu.VMEM((256, 512), F32),
             pltpu.VMEM((256, 512), BF),
             pltpu.VMEM((2, 16, 256), F32),
-            pltpu.VMEM((2, 3, 16, 256), F32),
-            pltpu.VMEM((2, 7, 16, 256), F32),
+            pltpu.VMEM((3, 2, 16, 256), F32),
+            pltpu.VMEM((7, 2, 16, 256), F32),
             pltpu.VMEM((2, 1024, 256), BF),
             pltpu.VMEM((3, 7, 128, 256), F32),
             pltpu.VMEM((3, 7, 128, 256), BF),
@@ -479,6 +490,15 @@
             collective_id=0, has_side_effects=True, vmem_limit_bytes=56 * 2**20
         ),
     )(x, g, ids.reshape(1, 256), w, ad.reshape(128, 512), au.reshape(128, 256))
+    mixed, hg, dg, ug = pl.pallas_call(
+        hand_over,
+        out_shape=shapes,
+        in_specs=[any_spec] * 4,
+        out_specs=(any_spec,) * 4,
+        scratch_shapes=[pltpu.VMEM(one.shape, one.dtype) for one in shapes]
+        + [pltpu.SemaphoreType.DMA((2, 11))],
+        compiler_params=pltpu.CompilerParams(vmem_limit_bytes=60 * 2**20),
+    )(*landed)
     return mixed, hg, dg.reshape(8, 16, 512), ug.reshape(8, 16, 256)
 
 

time: 78.4 us -> 68.6 us (0.87); the launches traced: 77 us -> 68.5 us
  local copies, waits for them, and re-layouts: 6.77 us -> 0 us
  Pallas kernels: 69.6 us -> 67.8 us
    unnamed x10 -> x0, local copies, waits for them, and re-layouts: 6.77 us -> none
    pallas_call x1 -> x2, Pallas kernels: 69.6 us -> 67.8 us  [the longest x1 63.6 us: on_device(): pl.pallas_call(kernel, out_shape=shapes, in_specs=[any_spec, any_spec, vm...]
where the time goes in v2:
time: 68.6 us; the launch traced here: 68.5 us
  Pallas kernels  67.8 us (99%)
    pallas_call x1, Pallas kernels, on_device(): pl.pallas_call(kernel, out_shape=shapes, in_specs=[any_spec, any_spec, vm...  63.6 us
    pallas_call x1, Pallas kernels, on_device(): pl.pallas_call(hand_over, out_shape=shapes, in_specs=[any_spec] * 4, out_...  4.17 us

profile of v2, /device:TPU:1, one launch (start us, length us, event | category | flops | bytes accessed | tf_op | source)
XLA Modules:
  0.0 68.5 jit_solution(557457480641191448)
XLA Ops:
  0.6 63.6 %shard_map.93 = (bf16[256,8192]{1,0:T(8,128)(2,1)}, bf16[256,512]{1,0:T(8,128)(2,1)}, f32[128,512]{1,0:T(8,128)}, f32[128,256]{1,0:T(8,128)}) custom-call(bf16[256,512]{1,0:T(8,128)(2,1)} %x_hbm.1, bf16[256,8192]{1,0:T(8,128)(2,1)} %g_hbm.1, s32[1,256]{1,0:T(1,128)} %bitcast.7, bf16[512,8192]{1,0:T(8,128)(2,1)} %w_hbm.1, bf16[128,512]{1,0:T(8,128)(2,1)} %bitcast.5, ...), custom_call_target="tpu_custom_call" | custom-call | tf_op jit(solution)/shard_map/pallas_call | solution.py:451
  64.3 4.2 %shard_map.94 = (bf16[256,8192]{1,0:T(8,128)(2,1)}, bf16[256,512]{1,0:T(8,128)(2,1)}, f32[128,512]{1,0:T(8,128)}, f32[128,256]{1,0:T(8,128)}) custom-call(bf16[256,8192]{1,0:T(8,128)(2,1)} %get-tuple-element.12.refs_0_, bf16[256,512]{1,0:T(8,128)(2,1)} %get-tuple-element.13.refs_1_, f32[128,512]{1,0:T(8,128)} %get-tuple-element.14.refs_2_, ...), custom_call_target="tpu_custom_call" | custom-call | tf_op jit(solution)/shard_map/pallas_call | solution.py:493

commit v3 on v2

--- a/solution.py
+++ b/solution.py
@@ -28,9 +28,9 @@
     x_hbm, g_hbm, ids_ref, w_hbm, ad_hbm, au_hbm,
     mixed, hg_out, dg_out, ug_out,
     xv, gs, gv, wv, adv, auv,
-    own, sib_tx, sib_rx, rs_tx, rs_rx, r_buf, p2_tx, p2_rx, fb,
+    own, sib_tx, sib_rx, rs_tx, rs_rx, r_buf, p2_tx, p2_rx, gat,
     hg_acc, hg_bf, lr_acc, lr_tx, lr_rx, sel, zr_own, zr_tx, zr_rx, dg_buf, ug_buf,
-    lsem, wsem, gsem, ssem, rsem,
+    lsem, wsem, gsem, osem, ssem, rsem,
 ):
     z = lax.axis_index("adapter")
     t = lax.axis_index("tensor")
@@ -142,17 +142,16 @@
         return send(hbm, view(z), zp), send(hbm, view(z), zm)
 
     def ag_next(view, prev, k):
+        last = k == 4
         prev[0].wait_recv()
+        if k < 5:
+            ref = view(slot(1 - k), TOP) if last else view(slot(1 - k))
+            hp = send(ref, ref, zp)
         prev[1].wait_recv()
-        if k == 5:
-            return None
-        if k == 4:
-            return (
-                send(view(slot(-3), TOP), view(slot(-3), TOP), zp),
-                send(view(slot(3), LOW), view(slot(3), LOW), zm),
-            )
-        a, b = slot(1 - k), slot(k - 1)
-        return send(view(a), view(a), zp), send(view(b), view(b), zm)
+        if k < 5:
+            ref = view(slot(k - 1), LOW) if last else view(slot(k - 1))
+            return hp, send(ref, ref, zm)
+        return None
 
     def sib_part(k):
         matmul_half(k, 0)
@@ -182,32 +181,32 @@
 
         lax.fori_loop(lo, hi, body, 0)
 
-    def psum_start(stage):
-        lr_tx[stage] = lr_acc[...]
-        src = lr_tx.at[stage]
+    def psum_start(which, stage):
+        lr_tx[which, stage] = lr_acc[which]
+        src = lr_tx.at[which, stage]
         if stage == 0:
-            return [send(src, lr_rx.at[0], sib)]
+            return [send(src, lr_rx.at[which, 0], sib)]
         at = at_x if stage == 1 else at_y
-        return [send(src, lr_rx.at[3 * stage - 3 + k], at(k)) for k in (1, 3, 2)]
-
-    def psum_end(stage, cps):
+        return [send(src, lr_rx.at[which, 3 * stage - 3 + k], at(k)) for k in (2, 1, 3)]
+
+    def psum_end(which, stage, cps):
         for cp in cps:
             cp.wait_recv()
         if stage == 0:
-            lr_acc[...] += lr_rx[0]
+            lr_acc[which] += lr_rx[which, 0]
         else:
             b = 3 * stage - 3
-            lr_acc[...] += lr_rx[b + 1] + lr_rx[b + 2] + lr_rx[b + 3]
+            lr_acc[which] += lr_rx[which, b + 1] + lr_rx[which, b + 2] + lr_rx[which, b + 3]
 
     h0 = ag_first(ad0, ad_hbm.at[:, pl.ds(0, 256)])
-    ld_w += [load_w(g) for g in range(2, 8)]
+    ld_w += [load_w(g) for g in range(2, 5)]
+    h1 = ag_first(ad1, ad_hbm.at[:, pl.ds(256, 256)])
     ld_x.wait()
     s0 = sib_part(0)
+    ld_w += [load_w(g) for g in range(5, 8)]
+    hu = ag_first(au0, au_hbm)
     matmul_half(0, 1)
-    h1 = ag_first(ad1, ad_hbm.at[:, pl.ds(256, 256)])
     s1 = sib_part(1)
-    matmul_half(1, 1)
-    hu = ag_first(au0, au_hbm)
     ld_ad = load(ad_hbm, adv.at[z], lsem.at[1])
     ld_au = load(au_hbm, auv.at[z], lsem.at[2])
     ld_gs = load(g_hbm.at[:, cols(t)], gs, lsem.at[3])
@@ -218,72 +217,79 @@
 
     s0.wait_recv()
     a0 = rs_send(0)
+    h0 = ag_next(ad0, h0, 2)
+    matmul_half(1, 1)
     s2 = sib_part(2)
-    h0 = ag_next(ad0, h0, 2)
-    matmul_half(2, 1)
+    h1 = ag_next(ad1, h1, 2)
     s1.wait_recv()
     a1 = rs_send(1)
-    h1 = ag_next(ad1, h1, 2)
-    s3 = sib_part(3)
+    matmul_half(2, 1)
+    hu = ag_next(au0, hu, 2)
     s2.wait_recv()
     a2 = rs_send(2)
-    hu = ag_next(au0, hu, 2)
+    s3 = sib_part(3)
+    h0 = ag_next(ad0, h0, 3)
     lr_acc[...] = jnp.zeros_like(lr_acc)
     ld_ad.wait()
+    project(0, z)
+    project(0, slot(1))
+    project(0, slot(7))
+    h1 = ag_next(ad1, h1, 3)
+    matmul_half(3, 1)
     ld_g = [load_g(g) for g in range(8)]
-    project(0, z)
-    h0 = ag_next(ad0, h0, 3)
-    matmul_half(3, 1)
-    project(0, slot(1))
-    h1 = ag_next(ad1, h1, 3)
+    hu = ag_next(au0, hu, 3)
+    project(0, slot(2))
+    project(0, slot(6))
+    h0 = ag_next(ad0, h0, 4)
     ld_au.wait()
     ld_gs.wait()
-    project(0, slot(7))
     project(1, z)
-    project(0, slot(2))
-    hu = ag_next(au0, hu, 3)
-    project(0, slot(6))
-    h0 = ag_next(ad0, h0, 4)
+    project(1, slot(1))
+    h1 = ag_next(ad1, h1, 4)
+    project(0, slot(3))
+    project(0, slot(5))
+    hu = ag_next(au0, hu, 4)
+    project(1, slot(7))
+    project(1, slot(2))
+    h0 = ag_next(ad0, h0, 5)
     s3.wait_recv()
     own[3] = own[3] + sib_rx[3].astype(F32)
-    h1 = ag_next(ad1, h1, 4)
-    project(1, slot(1))
-    project(1, slot(7))
-    project(0, slot(3))
-    hu = ag_next(au0, hu, 4)
-    project(0, slot(5))
-    h0 = ag_next(ad0, h0, 5)
-    project(1, slot(2))
-    project(1, slot(6))
     h1 = ag_next(ad1, h1, 5)
     project(0, slot(4))
+    lp = psum_start(0, 0)
+    project(1, slot(6))
     project(1, slot(3))
     project(1, slot(5))
     hu = ag_next(au0, hu, 5)
+    psum_end(0, 0, lp)
+    lp = psum_start(0, 1)
     project(1, slot(4))
-    lp = psum_start(0)
+    bp = psum_start(1, 0)
     a0.wait_recv()
     own[3] = own[3] + rs_rx[0].astype(F32)
-    psum_end(0, lp)
-    lp = psum_start(1)
+    psum_end(1, 0, bp)
+    bp = psum_start(1, 1)
     a1.wait_recv()
     a2.wait_recv()
-    r_buf[...] = own[3] + (rs_rx[1].astype(F32) + rs_rx[2].astype(F32))
     p2 = []
-    for k in (2, 1, 3):
-        p2_tx[k - 1] = r_buf[:, cols(lax.rem(q + k, 4))].astype(BF)
-        p2.append(send(p2_tx.at[k - 1], p2_rx.at[k - 1], at_q(k)))
+    for k in (2, 1, 3, 0):
+        at = cols(lax.rem(q + k, 4))
+        both = own[3, :, at] + (rs_rx[1, :, at].astype(F32) + rs_rx[2, :, at].astype(F32))
+        if k:
+            p2_tx[k - 1] = both.astype(BF)
+            p2.append(send(p2_tx.at[k - 1], p2_rx.at[k - 1], at_q(k)))
+        else:
+            r_buf[...] = both
+    psum_end(0, 1, lp)
+    lp = psum_start(0, 2)
     backward(0, 3, True)
-    psum_end(1, lp)
-    lp = psum_start(2)
-    backward(3, 8, False)
+    psum_end(1, 1, bp)
+    bp = psum_start(1, 2)
+    backward(3, 6, False)
     for cp in p2:
         cp.wait_recv()
-    r_buf[:, 0:256] = (
-        r_buf[:, cols(q)] + p2_rx[0].astype(F32) + p2_rx[1].astype(F32) + p2_rx[2].astype(F32)
-    )
-    psum_end(2, lp)
-
+    r_buf[...] = r_buf[...] + p2_rx[0].astype(F32) + p2_rx[1].astype(F32) + p2_rx[2].astype(F32)
+    psum_end(0, 2, lp)
     def select(which):
         low = lr_acc[which].astype(BF).astype(F32)[None]
         for s in range(8):
@@ -293,19 +299,28 @@
 
     select(0)
     adapted = tn(sel[0], auv[...].reshape(1024, 256))
-    fb[...] = (r_buf[:, 0:256] + adapted).astype(BF)
+    mine = tid(p, q, c)
+    gat[mine] = (r_buf[...] + adapted).astype(BF)
 
     def gather(block, device, rows=slice(None)):
-        ref = mixed.at[rows, cols(block)]
+        ref = gat.at[block, rows]
         return send(ref, ref, device)
 
-    mine = tid(p, q, c)
-    own_out = mixed.at[:, cols(mine)]
+    outs = []
+
+    def put_out(block):
+        outs.append(load(gat.at[block], mixed.at[:, cols(block)], osem.at[len(outs)]))
+
+    sibs = []
+
+    def finish(a, b):
+        block = tid(p + a, q + b, c)
+        sibs.append((gather(block, sib), tid(q + a, p + b, d)))
+        put_out(block)
+
     ag_p = {}
     ag_m = {}
-    ag_q = {k: send(fb, own_out, at_q(k)) for k in (1, 3, 2)}
-    sibs = []
-    ld_own = load(fb, own_out, lsem.at[4])
+    ag_q = {k: gather(mine, at_q(k)) for k in (1, 3, 2)}
 
     def grad_part(chain, s):
         rows = pl.ds(pl.multiple_of(s * 128, 128), 128)
@@ -352,11 +367,11 @@
         ag_p[k].wait_recv()
         bm = tid(p + 3, q + k, c)
         f1 = gather(bm, at_p(1), pl.ds(0, 128))
-        sibs.append(gather(bm, sib))
+        finish(3, k)
         ag_m[k].wait_recv()
         bq = tid(p + 1, q + k, c)
         f2 = gather(bq, at_p(3), pl.ds(128, 128))
-        sibs.append(gather(bq, sib))
+        finish(1, k)
         return f1, f2
 
     def pass_on(k):
@@ -364,23 +379,25 @@
         blk = tid(p, q + 4 - k, c)
         ag_p[4 - k] = gather(blk, at_p(1))
         ag_m[4 - k] = gather(blk, at_p(3))
-        sibs.append(gather(blk, sib))
+        finish(0, 4 - k)
 
     def to_sib(k):
         for cp in halves[k]:
             cp.wait_recv()
-        sibs.append(gather(tid(p + 2, q + k, c), sib))
+        finish(2, k)
 
     halves = {}
     cu = rs_start(0)
+    ag_p[0] = gather(mine, at_p(1))
+    ag_m[0] = gather(mine, at_p(3))
+    finish(0, 0)
+    psum_end(1, 2, bp)
     select(1)
-    ag_p[0] = send(fb, own_out, at_p(1))
-    ag_m[0] = send(fb, own_out, at_p(3))
-    sibs.append(send(fb, own_out, sib))
     c0 = rs_start(1)
     c1 = rs_start(2)
     for chain in range(3):
         rs_parts(chain, (3,))
+    backward(6, 8, False)
     cu = rs_next(0, 1, cu)
     halves[0] = spread(0)
     c0 = rs_next(1, 1, c0)
@@ -410,14 +427,15 @@
     to_sib(2)
     ug_buf[...] = rs_end(0, cu)
     st_ug = load(ug_buf, ug_out, lsem.at[6])
-    for cp in sibs:
+    for cp, block in sibs:
         cp.wait_recv()
+        put_out(block)
     dg_buf[:, 0:256] = rs_end(1, c0)
     dg_buf[:, 256:512] = rs_end(2, c1)
     st_dg = load(dg_buf, dg_out, lsem.at[7])
     for cp in sent:
         cp.wait_send()
-    for cp in (ld_own, st_hg, st_ug, st_dg):
+    for cp in outs + [st_hg, st_ug, st_dg]:
         cp.wait()
 
 
@@ -465,15 +483,15 @@
             pltpu.VMEM((4, 256, 1024), BF),
             pltpu.VMEM((3, 256, 1024), BF),
             pltpu.VMEM((3, 256, 1024), BF),
-            pltpu.VMEM((256, 1024), F32),
+            pltpu.VMEM((256, 256), F32),
             pltpu.VMEM((3, 256, 256), BF),
             pltpu.VMEM((3, 256, 256), BF),
-            pltpu.VMEM((256, 256), BF),
+            pltpu.VMEM((32, 256, 256), BF),
             pltpu.VMEM((256, 512), F32),
             pltpu.VMEM((256, 512), BF),
             pltpu.VMEM((2, 16, 256), F32),
-            pltpu.VMEM((3, 2, 16, 256), F32),
-            pltpu.VMEM((7, 2, 16, 256), F32),
+            pltpu.VMEM((2, 3, 16, 256), F32),
+            pltpu.VMEM((2, 7, 16, 256), F32),
             pltpu.VMEM((2, 1024, 256), BF),
             pltpu.VMEM((3, 7, 128, 256), F32),
             pltpu.VMEM((3, 7, 128, 256), BF),
@@ -481,6 +499,7 @@
             pltpu.VMEM((128, 512), F32),
             pltpu.VMEM((128, 256), F32),
             pltpu.SemaphoreType.DMA((8,)),
+            pltpu.SemaphoreType.DMA((32,)),
             pltpu.SemaphoreType.DMA((32,)),
             pltpu.SemaphoreType.DMA((32,)),
             pltpu.SemaphoreType.DMA((NSEM,)),

time: 68.6 us -> 65.6 us (0.956)
  Pallas kernels: 67.8 us -> 64.8 us
    pallas_call x1, Pallas kernels: 63.6 us -> 60.6 us  [on_device(): pl.pallas_call(kernel, out_shape=shapes, in_specs=[any_spec, any_spec, vm...]
where the time goes in v3:
time: 65.6 us; the launch traced here: 65.4 us
  Pallas kernels  64.8 us (99%)
    pallas_call x1, Pallas kernels, on_device(): pl.pallas_call(kernel, out_shape=shapes, in_specs=[any_spec, any_spec, vm...  60.6 us
    pallas_call x1, Pallas kernels, on_device(): pl.pallas_call(hand_over, out_shape=shapes, in_specs=[any_spec] * 4, out_...  4.17 us

profile of v3, /device:TPU:1, one launch (start us, length us, event | category | flops | bytes accessed | tf_op | source)
XLA Modules:
  0.0 65.4 jit_solution(14205875384345192840)
XLA Ops:
  0.6 60.6 %shard_map.93 = (bf16[256,8192]{1,0:T(8,128)(2,1)}, bf16[256,512]{1,0:T(8,128)(2,1)}, f32[128,512]{1,0:T(8,128)}, f32[128,256]{1,0:T(8,128)}) custom-call(bf16[256,512]{1,0:T(8,128)(2,1)} %x_hbm.1, bf16[256,8192]{1,0:T(8,128)(2,1)} %g_hbm.1, s32[1,256]{1,0:T(1,128)} %bitcast.7, bf16[512,8192]{1,0:T(8,128)(2,1)} %w_hbm.1, bf16[128,512]{1,0:T(8,128)(2,1)} %bitcast.5, ...), custom_call_target="tpu_custom_call" | custom-call | tf_op jit(solution)/shard_map/pallas_call | solution.py:469
  61.3 4.2 %shard_map.94 = (bf16[256,8192]{1,0:T(8,128)(2,1)}, bf16[256,512]{1,0:T(8,128)(2,1)}, f32[128,512]{1,0:T(8,128)}, f32[128,256]{1,0:T(8,128)}) custom-call(bf16[256,8192]{1,0:T(8,128)(2,1)} %get-tuple-element.12.refs_0_, bf16[256,512]{1,0:T(8,128)(2,1)} %get-tuple-element.13.refs_1_, f32[128,512]{1,0:T(8,128)} %get-tuple-element.14.refs_2_, ...), custom_call_target="tpu_custom_call" | custom-call | tf_op jit(solution)/shard_map/pallas_call | solution.py:512

commit v4 on v3

--- a/solution.py
+++ b/solution.py
@@ -320,7 +320,7 @@
 
     ag_p = {}
     ag_m = {}
-    ag_q = {k: gather(mine, at_q(k)) for k in (1, 3, 2)}
+    ag_q = {k: gather(mine, at_q(k)) for k in (2, 1, 3)}
 
     def grad_part(chain, s):
         rows = pl.ds(pl.multiple_of(s * 128, 128), 128)
@@ -388,8 +388,6 @@
 
     halves = {}
     cu = rs_start(0)
-    ag_p[0] = gather(mine, at_p(1))
-    ag_m[0] = gather(mine, at_p(3))
     finish(0, 0)
     psum_end(1, 2, bp)
     select(1)
@@ -397,14 +395,16 @@
     c1 = rs_start(2)
     for chain in range(3):
         rs_parts(chain, (3,))
+    ag_p[0] = gather(mine, at_p(1))
+    ag_m[0] = gather(mine, at_p(3))
     backward(6, 8, False)
     cu = rs_next(0, 1, cu)
-    halves[0] = spread(0)
-    c0 = rs_next(1, 1, c0)
-    c1 = rs_next(2, 1, c1)
     pass_on(1)
     pass_on(3)
     pass_on(2)
+    c0 = rs_next(1, 1, c0)
+    c1 = rs_next(2, 1, c1)
+    halves[0] = spread(0)
     for chain in range(3):
         rs_parts(chain, (2,))
     hg_bf[...] = (hg_acc[...] + tn(sel[1], adv[...].reshape(1024, 512))).astype(BF)

time: 65.6 us -> 69.2 us (1.055)
  Pallas kernels: 64.8 us -> 68.4 us
    pallas_call x1, Pallas kernels: 60.6 us -> 64.2 us  [on_device(): pl.pallas_call(kernel, out_shape=shapes, in_specs=[any_spec, any_spec, vm...]
where the time goes in v4:
time: 69.2 us; the launch traced here: 69.1 us
  Pallas kernels  68.4 us (99%)
    pallas_call x1, Pallas kernels, on_device(): pl.pallas_call(kernel, out_shape=shapes, in_specs=[any_spec, any_spec, vm...  64.2 us
    pallas_call x1, Pallas kernels, on_device(): pl.pallas_call(hand_over, out_shape=shapes, in_specs=[any_spec] * 4, out_...  4.17 us

profile of v4, /device:TPU:1, one launch (start us, length us, event | category | flops | bytes accessed | tf_op | source)
XLA Modules:
  0.0 69.1 jit_solution(5707368204212325103)
XLA Ops:
  0.6 64.2 %shard_map.93 = (bf16[256,8192]{1,0:T(8,128)(2,1)}, bf16[256,512]{1,0:T(8,128)(2,1)}, f32[128,512]{1,0:T(8,128)}, f32[128,256]{1,0:T(8,128)}) custom-call(bf16[256,512]{1,0:T(8,128)(2,1)} %x_hbm.1, bf16[256,8192]{1,0:T(8,128)(2,1)} %g_hbm.1, s32[1,256]{1,0:T(1,128)} %bitcast.7, bf16[512,8192]{1,0:T(8,128)(2,1)} %w_hbm.1, bf16[128,512]{1,0:T(8,128)(2,1)} %bitcast.5, ...), custom_call_target="tpu_custom_call" | custom-call | tf_op jit(solution)/shard_map/pallas_call | solution.py:469
  64.9 4.2 %shard_map.94 = (bf16[256,8192]{1,0:T(8,128)(2,1)}, bf16[256,512]{1,0:T(8,128)(2,1)}, f32[128,512]{1,0:T(8,128)}, f32[128,256]{1,0:T(8,128)}) custom-call(bf16[256,8192]{1,0:T(8,128)(2,1)} %get-tuple-element.12.refs_0_, bf16[256,512]{1,0:T(8,128)(2,1)} %get-tuple-element.13.refs_1_, f32[128,512]{1,0:T(8,128)} %get-tuple-element.14.refs_2_, ...), custom_call_target="tpu_custom_call" | custom-call | tf_op jit(solution)/shard_map/pallas_call | solution.py:512

commit v5 on v3

--- a/solution.py
+++ b/solution.py
@@ -318,8 +318,8 @@
         sibs.append((gather(block, sib), tid(q + a, p + b, d)))
         put_out(block)
 
-    ag_p = {}
-    ag_m = {}
+    ag_p = {0: gather(mine, at_p(1))}
+    ag_m = {0: gather(mine, at_p(3))}
     ag_q = {k: gather(mine, at_q(k)) for k in (1, 3, 2)}
 
     def grad_part(chain, s):
@@ -388,8 +388,6 @@
 
     halves = {}
     cu = rs_start(0)
-    ag_p[0] = gather(mine, at_p(1))
-    ag_m[0] = gather(mine, at_p(3))
     finish(0, 0)
     psum_end(1, 2, bp)
     select(1)

time: 65.6 us -> 65.7 us (level)
  no operation moved by 1% of the time
where the time goes in v5:
time: 65.7 us; the launch traced here: 65.6 us
  Pallas kernels  64.9 us (99%)
    pallas_call x1, Pallas kernels, on_device(): pl.pallas_call(kernel, out_shape=shapes, in_specs=[any_spec, any_spec, vm...  60.8 us
    pallas_call x1, Pallas kernels, on_device(): pl.pallas_call(hand_over, out_shape=shapes, in_specs=[any_spec] * 4, out_...  4.17 us

profile of v5, /device:TPU:1, one launch (start us, length us, event | category | flops | bytes accessed | tf_op | source)
XLA Modules:
  0.0 65.6 jit_solution(3733365463857640586)
XLA Ops:
  0.6 60.8 %shard_map.93 = (bf16[256,8192]{1,0:T(8,128)(2,1)}, bf16[256,512]{1,0:T(8,128)(2,1)}, f32[128,512]{1,0:T(8,128)}, f32[128,256]{1,0:T(8,128)}) custom-call(bf16[256,512]{1,0:T(8,128)(2,1)} %x_hbm.1, bf16[256,8192]{1,0:T(8,128)(2,1)} %g_hbm.1, s32[1,256]{1,0:T(1,128)} %bitcast.7, bf16[512,8192]{1,0:T(8,128)(2,1)} %w_hbm.1, bf16[128,512]{1,0:T(8,128)(2,1)} %bitcast.5, ...), custom_call_target="tpu_custom_call" | custom-call | tf_op jit(solution)/shard_map/pallas_call | solution.py:467
  61.4 4.2 %shard_map.94 = (bf16[256,8192]{1,0:T(8,128)(2,1)}, bf16[256,512]{1,0:T(8,128)(2,1)}, f32[128,512]{1,0:T(8,128)}, f32[128,256]{1,0:T(8,128)}) custom-call(bf16[256,8192]{1,0:T(8,128)(2,1)} %get-tuple-element.12.refs_0_, bf16[256,512]{1,0:T(8,128)(2,1)} %get-tuple-element.13.refs_1_, f32[128,512]{1,0:T(8,128)} %get-tuple-element.14.refs_2_, ...), custom_call_target="tpu_custom_call" | custom-call | tf_op jit(solution)/shard_map/pallas_call | solution.py:510
